TPU v7x, 512 devices: a whole 4x8x8 slice. The times are simulated.
512 devices in a mesh: section: 8 (over z_hi, x), dp: 64 (over y, z_lo, core).
Axes of the slice: x: 4, y: 8, z: 8 (z_hi: 2, z_lo: 4; z = z_hi * 4 + z_lo), core: 2. Of those that a mesh axis runs over, the one named last changes fastest.
Arguments:
- x_down: bfloat16 [8, 8192, 1024], P('section', 'dp'), may hold values from -16 to 16
- x_up: bfloat16 [8, 8192, 1024], P('section', 'dp'), may hold values from -16 to 16
- weights: bfloat16 [8, 2, 1024, 1024], P('section', None, 'dp'), as said below
- cot_down: bfloat16 [8192, 1024], P('dp'), may hold values from -6 to 6
- cot_up: bfloat16 [8192, 1024], P('dp'), may hold values from -6 to 6
Outputs:
- grad_down: bfloat16 [8, 8192, 1024], P('section', 'dp')
- grad_up: bfloat16 [8, 8192, 1024], P('section', 'dp')
- grad_w: float32 [8, 1024, 1024], P('section', 'dp')
Inputs may be any that keep to these rules, and one draw needn't show every extreme that they name: weights[j, 1] is the same matrix as weights[7 - j, 0].
All inputs are finite; a program needn't handle non-finite values.
Results may differ from a plain program's by a relative error of at most 0.009.
Values may be sent and summed in bfloat16 or wider, within the bound.
A program may use at most 64 MiB of HBM per device.

v0:
```python
import math

import jax
import jax.numpy as jnp
from jax import lax
from jax.sharding import PartitionSpec as P

MICRO = 4


def passed_along(value, axis, steps):
    count = lax.axis_size(axis)
    initial, last = (max(0, -steps), min(count, count - steps))
    return lax.ppermute(value, axis, [(source, source + steps) for source in range(initial, last)])


def swapped(x, axis, stride):
    return lax.ppermute(x, axis, [(i, i ^ 1 << stride) for i in range(lax.axis_size(axis))])


def gelu_slope(pre):
    cdf = 0.5 * (1.0 + lax.erf(pre * (1.0 / math.sqrt(2.0))))
    return cdf + pre * jnp.exp(-0.5 * pre * pre) * (1.0 / math.sqrt(2.0 * math.pi))


def section_back(pre, weight, upstream):
    delta = (gelu_slope(pre) * upstream.astype(jnp.float32)).astype(jnp.bfloat16)
    carried = lax.dot_general(
        delta, weight, (((1,), (1,)), ((), ())), preferred_element_type=jnp.float32
    )
    back = (upstream.astype(jnp.float32) + carried).astype(jnp.bfloat16)
    return (delta, back)


def per_device(x_down, x_up, weights, cot_down, cot_up):
    sections = lax.axis_size("section")
    here = lax.axis_index("section")
    pair = lax.all_gather(weights, "dp", axis=2, tiled=True)
    w_down = pair[0, 0]
    w_up = pair[0, 1]
    own_down = x_down[0]
    own_up = x_up[0]
    width = own_down.shape[1]
    micro = MICRO
    rows = own_down.shape[0] // micro
    down_blocks = own_down.reshape(micro, rows, width)
    up_blocks = own_up.reshape(micro, rows, width)
    cot_down_blocks = cot_down.reshape(micro, rows, width)
    cot_up_blocks = cot_up.reshape(micro, rows, width)

    def pre_down_of(index):
        block = lax.dynamic_index_in_dim(down_blocks, index, 0, keepdims=False)
        return jnp.dot(block, w_down, preferred_element_type=jnp.float32)

    def pre_up_of(index):
        block = lax.dynamic_index_in_dim(up_blocks, index, 0, keepdims=False)
        return jnp.dot(block, w_up, preferred_element_type=jnp.float32)

    def advance(tick, carry):
        recv_down, recv_up, out_down, out_up, del_down, del_up = carry
        slot_down = tick - (sections - 1 - here)
        slot_up = tick - here
        live_down = (slot_down >= 0) & (slot_down < micro)
        live_up = (slot_up >= 0) & (slot_up < micro)
        index_down = jnp.clip(slot_down, 0, micro - 1)
        index_up = jnp.clip(slot_up, 0, micro - 1)
        entry_down = lax.dynamic_index_in_dim(cot_down_blocks, index_down, 0, keepdims=False)
        entry_up = lax.dynamic_index_in_dim(cot_up_blocks, index_up, 0, keepdims=False)
        incoming_down = jnp.where(here == sections - 1, entry_down, recv_down)
        incoming_up = jnp.where(here == 0, entry_up, recv_up)
        delta_down, back_down = section_back(pre_down_of(index_down), w_down, incoming_down)
        delta_up, back_up = section_back(pre_up_of(index_up), w_up, incoming_up)
        out_down = jnp.where(
            live_down, lax.dynamic_update_index_in_dim(out_down, back_down, index_down, 0), out_down
        )
        del_down = jnp.where(
            live_down,
            lax.dynamic_update_index_in_dim(del_down, delta_down, index_down, 0),
            del_down,
        )
        out_up = jnp.where(
            live_up, lax.dynamic_update_index_in_dim(out_up, back_up, index_up, 0), out_up
        )
        del_up = jnp.where(
            live_up, lax.dynamic_update_index_in_dim(del_up, delta_up, index_up, 0), del_up
        )
        recv_down = passed_along(back_down, "section", -1)
        recv_up = passed_along(back_up, "section", 1)
        return (recv_down, recv_up, out_down, out_up, del_down, del_up)

    blank = jnp.zeros((rows, width), jnp.bfloat16)
    store = jnp.zeros((micro, rows, width), jnp.bfloat16)
    start = (blank, blank, store, store, store, store)
    final = lax.fori_loop(0, micro + sections - 1, advance, start)
    out_down, out_up, del_down, del_up = (final[2], final[3], final[4], final[5])
    up_deltas = del_up.reshape(rows * micro, width)
    arrived = jnp.stack([own_up, up_deltas])
    for level in range(sections.bit_length() - 1):
        arrived = swapped(arrived, "section", level)
    inputs_all = jnp.concatenate([own_down, arrived[0]], axis=0)
    deltas_all = jnp.concatenate([del_down.reshape(rows * micro, width), arrived[1]], axis=0)
    scale = 1.0 / math.sqrt(2.0 * own_down.shape[0] * lax.axis_size("dp"))
    local_grad = (
        lax.dot_general(
            inputs_all, deltas_all, (((0,), (0,)), ((), ())), preferred_element_type=jnp.float32
        )
        * scale
    )
    shared = lax.psum_scatter(local_grad, "dp", scatter_dimension=0, tiled=True)
    grad_down = out_down.reshape(1, rows * micro, width)
    grad_up = out_up.reshape(1, rows * micro, width)
    return (grad_down, grad_up, shared[None])


def solution(mesh):
    in_specs = (
        P("section", "dp", None),
        P("section", "dp", None),
        P("section", None, "dp", None),
        P("dp", None),
        P("dp", None),
    )
    out_specs = (P("section", "dp", None), P("section", "dp", None), P("section", "dp", None))
    return jax.shard_map(
        per_device, mesh=mesh, in_specs=in_specs, out_specs=out_specs, check_vma=False
    )
```

profile of v0, /device:TPU:6, one launch (start us, length us, event | category | flops | bytes accessed | tf_op | source)
XLA Modules:
  0.0 728.3 jit_solution(14401981026464822874)
XLA Ops:
  8.0 127.5 %all-gather.2.cloned.1.call-done = bf16[1,2,1024,1024]{3,2,1,0:T(8,128)(2,1)} async-done(((bf16[1,2,16,1024]{3,2,1,0:T(8,128)(2,1)}), bf16[1,2,1024,1024]{3,2,1,0:T(8,128)(2,1)}) %all-gather.2.cloned.1.call-update) | async-done | bytes 4194320 | tf_op jit(solution)/shard_map/all_gather | solution.py:38
  135.5 4.0 slice_bitcast_fusion
  141.1 248.4 %while.24 = (s32[]{:T(128)}, bf16[32,1024]{1,0:T(8,128)(2,1)S(1)}, bf16[32,1024]{1,0:T(8,128)(2,1)S(1)}, bf16[4,32,1024]{2,1,0:T(8,128)(2,1)}, bf16[4,32,1024]{2...) while((s32[]{:T(128)}, bf16[32,1024]{1,0:T(8,128)(2,1)S(1)}, ...), condition=%wide.region_1.2_spmd, body=%wide.region_0.1_spmd.sunk | while | flops 270401536 | bytes 19408284 | solution.py:94
  142.5 2.2 fusion.78
  144.7 5.9 collective-permute-start.1
  150.6 2.3 fusion.75
  152.9 2.2 fusion.76
  157.1 10.2 %collective-permute-done = bf16[32,1024]{1,0:T(8,128)(2,1)S(1)} collective-permute-done((bf16[32,1024]{1,0:T(8,128)(2,1)S(1)}, bf16[32,1024]{1,0:T(8,128)(2,1)S(1)}, u32[]{:S(2)}, u32[]{:S(2)}) %collective-permute-start) | collective-permute-done | bytes 65568 | tf_op jit(solution)/shard_map/while/body/eval_jaxpr/ppermute | solution.py:14
  168.7 2.2 fusion.78
  172.8 2.3 fusion.75
  175.1 2.2 fusion.76
  177.4 3.9 collective-permute-start
  181.3 8.3 %collective-permute-done = bf16[32,1024]{1,0:T(8,128)(2,1)S(1)} collective-permute-done((bf16[32,1024]{1,0:T(8,128)(2,1)S(1)}, bf16[32,1024]{1,0:T(8,128)(2,1)S(1)}, u32[]{:S(2)}, u32[]{:S(2)}) %collective-permute-start) | collective-permute-done | bytes 65568 | tf_op jit(solution)/shard_map/while/body/eval_jaxpr/ppermute | solution.py:14
  190.9 2.2 fusion.78
  195.1 2.3 fusion.75
  197.4 2.2 fusion.76
  199.6 3.9 collective-permute-start
  203.5 8.2 %collective-permute-done = bf16[32,1024]{1,0:T(8,128)(2,1)S(1)} collective-permute-done((bf16[32,1024]{1,0:T(8,128)(2,1)S(1)}, bf16[32,1024]{1,0:T(8,128)(2,1)S(1)}, u32[]{:S(2)}, u32[]{:S(2)}) %collective-permute-start) | collective-permute-done | bytes 65568 | tf_op jit(solution)/shard_map/while/body/eval_jaxpr/ppermute | solution.py:14
  213.1 2.2 fusion.78
  217.3 2.3 fusion.75
  219.6 2.2 fusion.76
  221.8 3.9 collective-permute-start
  225.8 8.2 %collective-permute-done = bf16[32,1024]{1,0:T(8,128)(2,1)S(1)} collective-permute-done((bf16[32,1024]{1,0:T(8,128)(2,1)S(1)}, bf16[32,1024]{1,0:T(8,128)(2,1)S(1)}, u32[]{:S(2)}, u32[]{:S(2)}) %collective-permute-start) | collective-permute-done | bytes 65568 | tf_op jit(solution)/shard_map/while/body/eval_jaxpr/ppermute | solution.py:14
  235.3 2.2 fusion.78
  239.5 2.3 fusion.75
  241.8 2.2 fusion.76
  244.0 3.9 collective-permute-start
  248.0 8.2 %collective-permute-done = bf16[32,1024]{1,0:T(8,128)(2,1)S(1)} collective-permute-done((bf16[32,1024]{1,0:T(8,128)(2,1)S(1)}, bf16[32,1024]{1,0:T(8,128)(2,1)S(1)}, u32[]{:S(2)}, u32[]{:S(2)}) %collective-permute-start) | collective-permute-done | bytes 65568 | tf_op jit(solution)/shard_map/while/body/eval_jaxpr/ppermute | solution.py:14
  257.6 2.2 fusion.78
  261.7 2.3 fusion.75
  264.0 2.2 fusion.76
  266.2 3.9 collective-permute-start
  270.2 8.2 %collective-permute-done = bf16[32,1024]{1,0:T(8,128)(2,1)S(1)} collective-permute-done((bf16[32,1024]{1,0:T(8,128)(2,1)S(1)}, bf16[32,1024]{1,0:T(8,128)(2,1)S(1)}, u32[]{:S(2)}, u32[]{:S(2)}) %collective-permute-start) | collective-permute-done | bytes 65568 | tf_op jit(solution)/shard_map/while/body/eval_jaxpr/ppermute | solution.py:14
  279.8 2.2 fusion.78
  283.9 2.3 fusion.75
  286.2 2.2 fusion.76
  288.4 3.9 collective-permute-start
  292.4 8.2 %collective-permute-done = bf16[32,1024]{1,0:T(8,128)(2,1)S(1)} collective-permute-done((bf16[32,1024]{1,0:T(8,128)(2,1)S(1)}, bf16[32,1024]{1,0:T(8,128)(2,1)S(1)}, u32[]{:S(2)}, u32[]{:S(2)}) %collective-permute-start) | collective-permute-done | bytes 65568 | tf_op jit(solution)/shard_map/while/body/eval_jaxpr/ppermute | solution.py:14
  302.0 2.2 fusion.78
  306.1 2.3 fusion.75
  308.4 2.2 fusion.76
  310.7 3.9 collective-permute-start
  314.6 8.2 %collective-permute-done = bf16[32,1024]{1,0:T(8,128)(2,1)S(1)} collective-permute-done((bf16[32,1024]{1,0:T(8,128)(2,1)S(1)}, bf16[32,1024]{1,0:T(8,128)(2,1)S(1)}, u32[]{:S(2)}, u32[]{:S(2)}) %collective-permute-start) | collective-permute-done | bytes 65568 | tf_op jit(solution)/shard_map/while/body/eval_jaxpr/ppermute | solution.py:14
  324.2 2.2 fusion.78
  328.3 2.3 fusion.75
  330.6 2.2 fusion.76
  332.9 3.9 collective-permute-start
  336.8 8.2 %collective-permute-done = bf16[32,1024]{1,0:T(8,128)(2,1)S(1)} collective-permute-done((bf16[32,1024]{1,0:T(8,128)(2,1)S(1)}, bf16[32,1024]{1,0:T(8,128)(2,1)S(1)}, u32[]{:S(2)}, u32[]{:S(2)}) %collective-permute-start) | collective-permute-done | bytes 65568 | tf_op jit(solution)/shard_map/while/body/eval_jaxpr/ppermute | solution.py:14
  346.4 2.2 fusion.78
  350.6 2.3 fusion.75
  352.9 2.2 fusion.76
  355.1 3.9 collective-permute-start
  359.0 8.2 %collective-permute-done = bf16[32,1024]{1,0:T(8,128)(2,1)S(1)} collective-permute-done((bf16[32,1024]{1,0:T(8,128)(2,1)S(1)}, bf16[32,1024]{1,0:T(8,128)(2,1)S(1)}, u32[]{:S(2)}, u32[]{:S(2)}) %collective-permute-start) | collective-permute-done | bytes 65568 | tf_op jit(solution)/shard_map/while/body/eval_jaxpr/ppermute | solution.py:14
  368.6 2.2 fusion.78
  372.8 2.3 fusion.75
  375.1 2.2 fusion.76
  377.3 3.9 collective-permute-start
  381.2 8.2 %collective-permute-done = bf16[32,1024]{1,0:T(8,128)(2,1)S(1)} collective-permute-done((bf16[32,1024]{1,0:T(8,128)(2,1)S(1)}, bf16[32,1024]{1,0:T(8,128)(2,1)S(1)}, u32[]{:S(2)}, u32[]{:S(2)}) %collective-permute-start) | collective-permute-done | bytes 65568 | tf_op jit(solution)/shard_map/while/body/eval_jaxpr/ppermute | solution.py:14
  390.5 1.9 collective-permute-start.2
  392.4 10.3 %collective-permute-done.2 = bf16[2,128,1024]{2,1,0:T(8,128)(2,1)S(1)} collective-permute-done((bf16[2,128,1024]{2,1,0:T(8,128)(2,1)S(1)}, bf16[2,128,1024]{2,1,0:T(8,128)(2,1)S(1)}, u32[]{:S(2)}, u32[]{:S(2)}) %collective-permute-start.2) | collective-permute-done | bytes 524320 | tf_op jit(solution)/shard_map/ppermute | solution.py:18
  404.7 10.7 %collective-permute-done.3 = bf16[2,128,1024]{2,1,0:T(8,128)(2,1)S(1)} collective-permute-done((bf16[2,128,1024]{2,1,0:T(8,128)(2,1)S(1)}, bf16[2,128,1024]{2,1,0:T(8,128)(2,1)S(1)}, u32[]{:S(2)}, u32[]{:S(2)}) %collective-permute-start.3) | collective-permute-done | bytes 524320 | tf_op jit(solution)/shard_map/ppermute | solution.py:18
  417.2 15.3 %collective-permute-done.4 = bf16[2,128,1024]{2,1,0:T(8,128)(2,1)S(1)} collective-permute-done((bf16[2,128,1024]{2,1,0:T(8,128)(2,1)S(1)}, bf16[2,128,1024]{2,1,0:T(8,128)(2,1)S(1)}, u32[]{:S(2)}, u32[]{:S(2)}) %collective-permute-start.4) | collective-permute-done | bytes 524320 | tf_op jit(solution)/shard_map/ppermute | solution.py:18
  432.6 2.7 convolution_multiply_fusion
  435.3 286.1 %reduce-scatter.2.cloned.1.call-done = f32[16,1024]{1,0:T(8,128)} async-done(((f32[1024,1024]{1,0:T(8,128)}), f32[16,1024]{1,0:T(8,128)}) %reduce-scatter.2.cloned.1.call-update) | async-done | bytes 65552 | tf_op jit(solution)/shard_map/reduce_scatter | solution.py:109
  (75 shorter events, 43.2 us)
Async XLA Ops:
  7.2 128.3 %all-gather.2.cloned.1.call-start = ((), (), s32[]{:S(2)}) async-start(), calls=%async_computation.1 | async-start | bytes 4259840 | tf_op jit(solution)/shard_map/all_gather | solution.py:38
  7.9 713.6 %reduce-scatter.2.cloned.1.call-start = ((), (), s32[]{:S(2)}) async-start(), calls=%async_computation.2 | async-start | bytes 4259840 | tf_op jit(solution)/shard_map/reduce_scatter | solution.py:109
  8.0 133.1 %copy-start.1 = (bf16[128,1024]{1,0:T(8,128)(2,1)S(1)}, bf16[128,1024]{1,0:T(8,128)(2,1)}, u32[]{:S(2)}) copy-start(bf16[128,1024]{1,0:T(8,128)(2,1)} %param.10) | copy-start | bytes 786436
  8.0 133.1 %copy-start.2 = (bf16[128,1024]{1,0:T(8,128)(2,1)S(1)}, bf16[128,1024]{1,0:T(8,128)(2,1)}, u32[]{:S(2)}) copy-start(bf16[128,1024]{1,0:T(8,128)(2,1)} %param.11) | copy-start | bytes 786436
  144.7 12.4 %collective-permute-start.1 = (bf16[32,1024]{1,0:T(8,128)(2,1)S(1)}, bf16[32,1024]{1,0:T(8,128)(2,1)S(1)}, u32[]{:S(2)}, u32[]{:S(2)}) collective-permute-start(bf16[32,1024]{1,0:T(8,128)(2,1)S(1)} %get-tuple-element.466), channel_id=1, source_target_pairs={{0,64},{64,128},{128,192},{192,256},{256,320},{320,384},{384,448},... | collective-permute-start | bytes 196616 | tf_op jit(solution)/shard_map/while/body/eval_jaxpr/ppermute | solution.py:14
  150.6 2.3 copy-start
  155.1 12.2 %collective-permute-start = (bf16[32,1024]{1,0:T(8,128)(2,1)S(1)}, bf16[32,1024]{1,0:T(8,128)(2,1)S(1)}, u32[]{:S(2)}, u32[]{:S(2)}) collective-permute-start(bf16[32,1024]{1,0:T(8,128)(2,1)S(1)} %get-tuple-element.464), channel_id=1, source_target_pairs={{64,0},{128,64},{192,128},{256,192},{320,256},{384,320},{448,384},... | collective-permute-start | bytes 196616 | tf_op jit(solution)/shard_map/while/body/eval_jaxpr/ppermute | solution.py:14
  170.9 10.4 %collective-permute-start.1 = (bf16[32,1024]{1,0:T(8,128)(2,1)S(1)}, bf16[32,1024]{1,0:T(8,128)(2,1)S(1)}, u32[]{:S(2)}, u32[]{:S(2)}) collective-permute-start(bf16[32,1024]{1,0:T(8,128)(2,1)S(1)} %get-tuple-element.466), channel_id=1, source_target_pairs={{0,64},{64,128},{128,192},{192,256},{256,320},{320,384},{384,448},... | collective-permute-start | bytes 196616 | tf_op jit(solution)/shard_map/while/body/eval_jaxpr/ppermute | solution.py:14
  172.8 2.3 copy-start
  177.4 12.2 %collective-permute-start = (bf16[32,1024]{1,0:T(8,128)(2,1)S(1)}, bf16[32,1024]{1,0:T(8,128)(2,1)S(1)}, u32[]{:S(2)}, u32[]{:S(2)}) collective-permute-start(bf16[32,1024]{1,0:T(8,128)(2,1)S(1)} %get-tuple-element.464), channel_id=1, source_target_pairs={{64,0},{128,64},{192,128},{256,192},{320,256},{384,320},{448,384},... | collective-permute-start | bytes 196616 | tf_op jit(solution)/shard_map/while/body/eval_jaxpr/ppermute | solution.py:14
  193.1 10.4 %collective-permute-start.1 = (bf16[32,1024]{1,0:T(8,128)(2,1)S(1)}, bf16[32,1024]{1,0:T(8,128)(2,1)S(1)}, u32[]{:S(2)}, u32[]{:S(2)}) collective-permute-start(bf16[32,1024]{1,0:T(8,128)(2,1)S(1)} %get-tuple-element.466), channel_id=1, source_target_pairs={{0,64},{64,128},{128,192},{192,256},{256,320},{320,384},{384,448},... | collective-permute-start | bytes 196616 | tf_op jit(solution)/shard_map/while/body/eval_jaxpr/ppermute | solution.py:14
  195.1 2.3 copy-start
  199.6 12.2 %collective-permute-start = (bf16[32,1024]{1,0:T(8,128)(2,1)S(1)}, bf16[32,1024]{1,0:T(8,128)(2,1)S(1)}, u32[]{:S(2)}, u32[]{:S(2)}) collective-permute-start(bf16[32,1024]{1,0:T(8,128)(2,1)S(1)} %get-tuple-element.464), channel_id=1, source_target_pairs={{64,0},{128,64},{192,128},{256,192},{320,256},{384,320},{448,384},... | collective-permute-start | bytes 196616 | tf_op jit(solution)/shard_map/while/body/eval_jaxpr/ppermute | solution.py:14
  215.4 10.4 %collective-permute-start.1 = (bf16[32,1024]{1,0:T(8,128)(2,1)S(1)}, bf16[32,1024]{1,0:T(8,128)(2,1)S(1)}, u32[]{:S(2)}, u32[]{:S(2)}) collective-permute-start(bf16[32,1024]{1,0:T(8,128)(2,1)S(1)} %get-tuple-element.466), channel_id=1, source_target_pairs={{0,64},{64,128},{128,192},{192,256},{256,320},{320,384},{384,448},... | collective-permute-start | bytes 196616 | tf_op jit(solution)/shard_map/while/body/eval_jaxpr/ppermute | solution.py:14
  217.3 2.3 copy-start
  221.8 12.2 %collective-permute-start = (bf16[32,1024]{1,0:T(8,128)(2,1)S(1)}, bf16[32,1024]{1,0:T(8,128)(2,1)S(1)}, u32[]{:S(2)}, u32[]{:S(2)}) collective-permute-start(bf16[32,1024]{1,0:T(8,128)(2,1)S(1)} %get-tuple-element.464), channel_id=1, source_target_pairs={{64,0},{128,64},{192,128},{256,192},{320,256},{384,320},{448,384},... | collective-permute-start | bytes 196616 | tf_op jit(solution)/shard_map/while/body/eval_jaxpr/ppermute | solution.py:14
  237.6 10.4 %collective-permute-start.1 = (bf16[32,1024]{1,0:T(8,128)(2,1)S(1)}, bf16[32,1024]{1,0:T(8,128)(2,1)S(1)}, u32[]{:S(2)}, u32[]{:S(2)}) collective-permute-start(bf16[32,1024]{1,0:T(8,128)(2,1)S(1)} %get-tuple-element.466), channel_id=1, source_target_pairs={{0,64},{64,128},{128,192},{192,256},{256,320},{320,384},{384,448},... | collective-permute-start | bytes 196616 | tf_op jit(solution)/shard_map/while/body/eval_jaxpr/ppermute | solution.py:14
  239.5 2.3 copy-start
  244.0 12.2 %collective-permute-start = (bf16[32,1024]{1,0:T(8,128)(2,1)S(1)}, bf16[32,1024]{1,0:T(8,128)(2,1)S(1)}, u32[]{:S(2)}, u32[]{:S(2)}) collective-permute-start(bf16[32,1024]{1,0:T(8,128)(2,1)S(1)} %get-tuple-element.464), channel_id=1, source_target_pairs={{64,0},{128,64},{192,128},{256,192},{320,256},{384,320},{448,384},... | collective-permute-start | bytes 196616 | tf_op jit(solution)/shard_map/while/body/eval_jaxpr/ppermute | solution.py:14
  259.8 10.4 %collective-permute-start.1 = (bf16[32,1024]{1,0:T(8,128)(2,1)S(1)}, bf16[32,1024]{1,0:T(8,128)(2,1)S(1)}, u32[]{:S(2)}, u32[]{:S(2)}) collective-permute-start(bf16[32,1024]{1,0:T(8,128)(2,1)S(1)} %get-tuple-element.466), channel_id=1, source_target_pairs={{0,64},{64,128},{128,192},{192,256},{256,320},{320,384},{384,448},... | collective-permute-start | bytes 196616 | tf_op jit(solution)/shard_map/while/body/eval_jaxpr/ppermute | solution.py:14
  261.7 2.3 copy-start
  266.2 12.2 %collective-permute-start = (bf16[32,1024]{1,0:T(8,128)(2,1)S(1)}, bf16[32,1024]{1,0:T(8,128)(2,1)S(1)}, u32[]{:S(2)}, u32[]{:S(2)}) collective-permute-start(bf16[32,1024]{1,0:T(8,128)(2,1)S(1)} %get-tuple-element.464), channel_id=1, source_target_pairs={{64,0},{128,64},{192,128},{256,192},{320,256},{384,320},{448,384},... | collective-permute-start | bytes 196616 | tf_op jit(solution)/shard_map/while/body/eval_jaxpr/ppermute | solution.py:14
  282.0 10.4 %collective-permute-start.1 = (bf16[32,1024]{1,0:T(8,128)(2,1)S(1)}, bf16[32,1024]{1,0:T(8,128)(2,1)S(1)}, u32[]{:S(2)}, u32[]{:S(2)}) collective-permute-start(bf16[32,1024]{1,0:T(8,128)(2,1)S(1)} %get-tuple-element.466), channel_id=1, source_target_pairs={{0,64},{64,128},{128,192},{192,256},{256,320},{320,384},{384,448},... | collective-permute-start | bytes 196616 | tf_op jit(solution)/shard_map/while/body/eval_jaxpr/ppermute | solution.py:14
  283.9 2.3 copy-start
  288.4 12.2 %collective-permute-start = (bf16[32,1024]{1,0:T(8,128)(2,1)S(1)}, bf16[32,1024]{1,0:T(8,128)(2,1)S(1)}, u32[]{:S(2)}, u32[]{:S(2)}) collective-permute-start(bf16[32,1024]{1,0:T(8,128)(2,1)S(1)} %get-tuple-element.464), channel_id=1, source_target_pairs={{64,0},{128,64},{192,128},{256,192},{320,256},{384,320},{448,384},... | collective-permute-start | bytes 196616 | tf_op jit(solution)/shard_map/while/body/eval_jaxpr/ppermute | solution.py:14
  304.2 10.4 %collective-permute-start.1 = (bf16[32,1024]{1,0:T(8,128)(2,1)S(1)}, bf16[32,1024]{1,0:T(8,128)(2,1)S(1)}, u32[]{:S(2)}, u32[]{:S(2)}) collective-permute-start(bf16[32,1024]{1,0:T(8,128)(2,1)S(1)} %get-tuple-element.466), channel_id=1, source_target_pairs={{0,64},{64,128},{128,192},{192,256},{256,320},{320,384},{384,448},... | collective-permute-start | bytes 196616 | tf_op jit(solution)/shard_map/while/body/eval_jaxpr/ppermute | solution.py:14
  306.1 2.3 copy-start
  310.7 12.2 %collective-permute-start = (bf16[32,1024]{1,0:T(8,128)(2,1)S(1)}, bf16[32,1024]{1,0:T(8,128)(2,1)S(1)}, u32[]{:S(2)}, u32[]{:S(2)}) collective-permute-start(bf16[32,1024]{1,0:T(8,128)(2,1)S(1)} %get-tuple-element.464), channel_id=1, source_target_pairs={{64,0},{128,64},{192,128},{256,192},{320,256},{384,320},{448,384},... | collective-permute-start | bytes 196616 | tf_op jit(solution)/shard_map/while/body/eval_jaxpr/ppermute | solution.py:14
  326.4 10.4 %collective-permute-start.1 = (bf16[32,1024]{1,0:T(8,128)(2,1)S(1)}, bf16[32,1024]{1,0:T(8,128)(2,1)S(1)}, u32[]{:S(2)}, u32[]{:S(2)}) collective-permute-start(bf16[32,1024]{1,0:T(8,128)(2,1)S(1)} %get-tuple-element.466), channel_id=1, source_target_pairs={{0,64},{64,128},{128,192},{192,256},{256,320},{320,384},{384,448},... | collective-permute-start | bytes 196616 | tf_op jit(solution)/shard_map/while/body/eval_jaxpr/ppermute | solution.py:14
  328.3 2.3 copy-start
  332.9 12.2 %collective-permute-start = (bf16[32,1024]{1,0:T(8,128)(2,1)S(1)}, bf16[32,1024]{1,0:T(8,128)(2,1)S(1)}, u32[]{:S(2)}, u32[]{:S(2)}) collective-permute-start(bf16[32,1024]{1,0:T(8,128)(2,1)S(1)} %get-tuple-element.464), channel_id=1, source_target_pairs={{64,0},{128,64},{192,128},{256,192},{320,256},{384,320},{448,384},... | collective-permute-start | bytes 196616 | tf_op jit(solution)/shard_map/while/body/eval_jaxpr/ppermute | solution.py:14
  348.6 10.4 %collective-permute-start.1 = (bf16[32,1024]{1,0:T(8,128)(2,1)S(1)}, bf16[32,1024]{1,0:T(8,128)(2,1)S(1)}, u32[]{:S(2)}, u32[]{:S(2)}) collective-permute-start(bf16[32,1024]{1,0:T(8,128)(2,1)S(1)} %get-tuple-element.466), channel_id=1, source_target_pairs={{0,64},{64,128},{128,192},{192,256},{256,320},{320,384},{384,448},... | collective-permute-start | bytes 196616 | tf_op jit(solution)/shard_map/while/body/eval_jaxpr/ppermute | solution.py:14
  350.5 2.3 copy-start
  355.1 12.2 %collective-permute-start = (bf16[32,1024]{1,0:T(8,128)(2,1)S(1)}, bf16[32,1024]{1,0:T(8,128)(2,1)S(1)}, u32[]{:S(2)}, u32[]{:S(2)}) collective-permute-start(bf16[32,1024]{1,0:T(8,128)(2,1)S(1)} %get-tuple-element.464), channel_id=1, source_target_pairs={{64,0},{128,64},{192,128},{256,192},{320,256},{384,320},{448,384},... | collective-permute-start | bytes 196616 | tf_op jit(solution)/shard_map/while/body/eval_jaxpr/ppermute | solution.py:14
  370.8 10.4 %collective-permute-start.1 = (bf16[32,1024]{1,0:T(8,128)(2,1)S(1)}, bf16[32,1024]{1,0:T(8,128)(2,1)S(1)}, u32[]{:S(2)}, u32[]{:S(2)}) collective-permute-start(bf16[32,1024]{1,0:T(8,128)(2,1)S(1)} %get-tuple-element.466), channel_id=1, source_target_pairs={{0,64},{64,128},{128,192},{192,256},{256,320},{320,384},{384,448},... | collective-permute-start | bytes 196616 | tf_op jit(solution)/shard_map/while/body/eval_jaxpr/ppermute | solution.py:14
  372.7 2.3 copy-start
  377.3 12.2 %collective-permute-start = (bf16[32,1024]{1,0:T(8,128)(2,1)S(1)}, bf16[32,1024]{1,0:T(8,128)(2,1)S(1)}, u32[]{:S(2)}, u32[]{:S(2)}) collective-permute-start(bf16[32,1024]{1,0:T(8,128)(2,1)S(1)} %get-tuple-element.464), channel_id=1, source_target_pairs={{64,0},{128,64},{192,128},{256,192},{320,256},{384,320},{448,384},... | collective-permute-start | bytes 196616 | tf_op jit(solution)/shard_map/while/body/eval_jaxpr/ppermute | solution.py:14
  389.5 43.2 %copy-start.3 = (bf16[4,32,1024]{2,1,0:T(8,128)(2,1)S(1)}, bf16[4,32,1024]{2,1,0:T(8,128)(2,1)}, u32[]{:S(2)}) copy-start(bf16[4,32,1024]{2,1,0:T(8,128)(2,1)} %get-tuple-element.543) | copy-start | bytes 786436
  390.5 12.2 %collective-permute-start.2 = (bf16[2,128,1024]{2,1,0:T(8,128)(2,1)S(1)}, bf16[2,128,1024]{2,1,0:T(8,128)(2,1)S(1)}, u32[]{:S(2)}, u32[]{:S(2)}) collective-permute-start(bf16[2,128,1024]{2,1,0:T(8,128)(2,1)S(1)} %pad_maximum_fusion), channel_id=1, source_target_pairs={{0,64},{64,0},{128,192},{192,128},{256,320},{320,256},{384,448},{4... | collective-permute-start | bytes 1572872 | tf_op jit(solution)/shard_map/ppermute | solution.py:18
  402.7 12.6 %collective-permute-start.3 = (bf16[2,128,1024]{2,1,0:T(8,128)(2,1)S(1)}, bf16[2,128,1024]{2,1,0:T(8,128)(2,1)S(1)}, u32[]{:S(2)}, u32[]{:S(2)}) collective-permute-start(bf16[2,128,1024]{2,1,0:T(8,128)(2,1)S(1)} %collective-permute-done.2), channel_id=1, source_target_pairs={{0,128},{64,192},{128,0},{192,64},{256,384},{320,448},{384,256},{4... | collective-permute-start | bytes 1572872 | tf_op jit(solution)/shard_map/ppermute | solution.py:18
  415.3 17.3 %collective-permute-start.4 = (bf16[2,128,1024]{2,1,0:T(8,128)(2,1)S(1)}, bf16[2,128,1024]{2,1,0:T(8,128)(2,1)S(1)}, u32[]{:S(2)}, u32[]{:S(2)}) collective-permute-start(bf16[2,128,1024]{2,1,0:T(8,128)(2,1)S(1)} %collective-permute-done.3), channel_id=1, source_target_pairs={{0,256},{64,320},{128,384},{192,448},{256,0},{320,64},{384,128},{4... | collective-permute-start | bytes 1572872 | tf_op jit(solution)/shard_map/ppermute | solution.py:18
Sparse Core Ops, SparseCore 0:
  10.2 125.2 all-gather.1
  435.5 285.9 reduce-scatter.1
where the time goes:
time: 731 us; the launch traced here: 728 us
  waiting for transfers between devices  543 us (74%)
  matrix products  91.6 us (13%)
  starting transfers between devices  71.8 us (10%)
  between operations  14.1 us (2%)
    reduce_scatter x1, waiting for transfers between devices, per_device(): shared = lax.psum_scatter(local_grad, 'dp', scatter_dimension=0, tiled=True)  286 us
    all_gather x1, waiting for transfers between devices, per_device(): pair = lax.all_gather(weights, 'dp', axis=2, tiled=True)  128 us
    ppermute x22, waiting for transfers between devices, passed_along(): lax.ppermute(value, axis, [(source, source + steps) for source in range(i...  92.6 us
    ppermute x22, starting transfers between devices, passed_along(): lax.ppermute(value, axis, [(source, source + steps) for source in range(i...  66 us
    dot_general x22, matrix products, section_back(): lax.dot_general(delta, weight, (((1,), (1,)), ((), ())), preferred_elemen...  48.8 us
    ppermute x3, waiting for transfers between devices, swapped(): lax.ppermute(x, axis, [(i, i ^ 1 << stride) for i in range(lax.axis_size(...  36.3 us
    dot_general x11, matrix products, pre_down_of(): return jnp.dot(block, w_down, preferred_element_type=jnp.float32)  25.2 us
    dot_general x11, matrix products, pre_up_of(): return jnp.dot(block, w_up, preferred_element_type=jnp.float32)  14.9 us
  transfers between devices with their start and end apart: 27, of which 16 were waited for; matrix products, arithmetic and copies ran while one was open for 7% of the time, Pallas kernels for 0%

commit v1 on v0

v1 whole, which is shorter than its diff:
```python
import functools
import math

import jax
import jax.numpy as jnp
from jax import lax
from jax.experimental import pallas as pl
from jax.experimental.pallas import tpu as pltpu
from jax.sharding import PartitionSpec as P

Y, Z, C = 8, 4, 2
SECTIONS = 8
D = 1024
H = D // 2
ROWS = 128
SHARD = 16
MICRO = 4
STEP = ROWS // MICRO
HALF = ((0, 1), (2, 3))
MESH = pl.DeviceIdType.MESH
F32, BF16 = jnp.float32, jnp.bfloat16


def gelu_slope(pre):
    cdf = 0.5 * (1.0 + lax.erf(pre * (1.0 / math.sqrt(2.0))))
    return cdf + pre * jnp.exp(-0.5 * pre * pre) * (1.0 / math.sqrt(2.0 * math.pi))


def kernel(
    x_down, x_up, weights, cot_down, cot_up, grad_down, grad_up, grad_w,
    w, x, g_in, g_out, slope, delta, part, y_in, y_own, z_out, z_in, total, far_out, far_in, gw,
    load_sem, out_sem,
    agz_s, agz_r, agy_s, agy_r, agc_s, agc_r,
    xc_s, xc_r, ch_s, ch_r, dc_s, dc_r,
    rsy_s, rsy_r, rsz_s, rsz_r, far_s, far_r,
):
    s = lax.axis_index("section")
    me = lax.axis_index("dp")
    y, z, c = me // (Z * C), (me // C) % Z, me % C
    hi = s // (SECTIONS // 2)
    p = s + hi * (SECTIONS - 1 - 2 * s)
    ahead = 1 - 2 * hi

    def dev(ss, yy, zz, cc):
        return (ss, (yy * Z + zz) * C + cc)

    def send(src, dst, send_sem, recv_sem, to):
        return pltpu.make_async_remote_copy(
            src_ref=src, dst_ref=dst, send_sem=send_sem, recv_sem=recv_sem,
            device_id=to, device_id_type=MESH,
        )

    sibling = dev(s, y, z, 1 - c)

    def y_at(step):
        return (y + step + 2 * Y) % Y

    def z_at(step):
        return (z + step + 2 * Z) % Z

    def loads():
        @pl.when(hi == 1)
        def _():
            pltpu.make_async_copy(x_down, x.at[0, c], load_sem.at[0]).start()
            pltpu.make_async_copy(x_up, x.at[1, c], load_sem.at[1]).start()

        @pl.when(hi == 0)
        def _():
            pltpu.make_async_copy(x_up, x.at[0, c], load_sem.at[0]).start()
            pltpu.make_async_copy(x_down, x.at[1, c], load_sem.at[1]).start()

        for i in range(MICRO):
            rows = pl.ds(i * STEP, STEP)

            @pl.when(s == SECTIONS - 1)
            def _():
                pltpu.make_async_copy(cot_down.at[rows], g_in.at[0, rows], ch_r.at[0, i]).start()

            @pl.when(s == 0)
            def _():
                pltpu.make_async_copy(cot_up.at[rows], g_in.at[0, rows], ch_r.at[0, i]).start()

    def own_weight(r):
        index = 1 - hi if r == 0 else hi
        return pltpu.make_async_copy(weights.at[index], w.at[r, y, z, c], load_sem.at[2 + r])

    def agz(r, k):
        block = w.at[r, y, z, c]
        return send(block, block, agz_s.at[r, k - 1], agz_r.at[r, k - 1], dev(s, y, z_at(k), c))

    def agz_in(r, k):
        block = w.at[r, y, z_at(-k), c]
        return send(block, block, agz_s.at[r, k - 1], agz_r.at[r, k - 1], dev(s, y, z_at(k), c))

    def agy(r, d, t, j, arriving=False):
        sign = 1 - 2 * d
        block = w.at[r, y_at(-sign * (t + 1 if arriving else t)), z_at(-j), c]
        to = dev(s, y_at(sign), z, c)
        return send(block, block, agy_s.at[r, d, t, j], agy_r.at[r, d, t, j], to)

    def agc(r, k, arriving=False):
        origin = (1, 2, 3, -1, -2, -3, 0, 4)[k]
        block = w.at[r, y_at(-origin), :, 1 - c if arriving else c]
        return send(block, block, agc_s.at[r, k], agc_r.at[r, k], sibling)

    def ag_z_start(r):
        own_weight(r).wait()
        for k in range(1, Z):
            agz(r, k).start()

    def ag_y_start(r):
        for j in range(Z):
            if j:
                agz_in(r, j).wait_recv()
            for d in range(2):
                agy(r, d, 0, j).start()
        agc(r, 6).start()

    def ag_y_forward(r):
        for t in range(1, 4):
            for j in range(Z):
                for d in range(2):
                    agy(r, d, t - 1, j, True).wait_recv()
                    if t < 3 or j in HALF[d]:
                        agy(r, d, t, j).start()
            for d in range(2):
                agc(r, d * 3 + t - 1).start()
        for d in range(2):
            for j in HALF[d]:
                agy(r, d, 3, j, True).wait_recv()
        agc(r, 7).start()

    def ag_sends_done(r):
        for k in range(1, Z):
            agz(r, k).wait_send()
        for d in range(2):
            for t in range(4):
                for j in range(Z):
                    if t < 3 or j in HALF[d]:
                        agy(r, d, t, j).wait_send()
        for k in range(8):
            agc(r, k).wait_send()

    def weight(r):
        return w[r].reshape(D, D)

    def prepare(r):
        for k in range(8):
            agc(r, k, True).wait_recv()
        pre = jnp.dot(x[r, c], weight(r), preferred_element_type=F32)
        slope[r] = gelu_slope(pre)

    def dc(r, i, arriving=False):
        block = delta.at[r, 1 - c, c, pl.ds(i * STEP, STEP)] if arriving else delta.at[r, c, 1 - c, pl.ds(i * STEP, STEP)]
        return send(block, block, dc_s.at[r, i], dc_r.at[r, i], sibling)

    def hop(r, i):
        rows = pl.ds(i * STEP, STEP)
        if r == 0:
            slot, to = p // 3, dev(s + ahead, y, z, c)
        else:
            slot, to = 1, dev(s - ahead, y, z, c)
        return send(g_out.at[r, rows], g_in.at[slot, rows], ch_s.at[r, i], ch_r.at[slot, i], to)

    def hop_in(r, i):
        rows = pl.ds(i * STEP, STEP)
        return pltpu.make_async_copy(g_out.at[r, rows], g_in.at[r, rows], ch_r.at[r, i])

    def chain(r):
        for i in range(MICRO):
            rows = pl.ds(i * STEP, STEP)
            hop_in(r, i).wait()
            g = g_in[r, rows, :].astype(F32)
            d = (slope[r, rows, :] * g).astype(BF16)
            delta[r, c, 0, rows, :] = d[:, :H]
            delta[r, c, 1, rows, :] = d[:, H:]
            dc(r, i).start()
            carried = lax.dot_general(
                d, weight(r), (((1,), (1,)), ((), ())), preferred_element_type=F32
            )
            g_out[r, rows, :] = (g + carried).astype(BF16)
            if r == 0:
                hop(r, i).start()
            else:
                pl.when(p > 0)(hop(r, i).start)

    def store_grads(r, wait=False):
        if wait:
            pltpu.make_async_copy(g_out.at[r], grad_down, out_sem.at[r]).wait()
            return
        for value in range(2):
            out = grad_down if value != r else grad_up
            pl.when(hi == value)(pltpu.make_async_copy(g_out.at[r], out, out_sem.at[r]).start)

    def xc(r, arriving=False):
        block = x.at[r, 1 - c if arriving else c]
        return send(block, block, xc_s.at[r], xc_r.at[r], sibling)

    def rsy(r, d, t, q, arriving=False):
        sign = 1 - 2 * d
        if t == 0 or (t == 1 and q not in HALF[d]):
            src = y_own.at[r, d, q]
        else:
            src = y_in.at[r, d, t - 1, q]
        dst = y_in.at[r, d, t, q]
        to = dev(s, y_at(sign), z, c)
        return send(src, dst, rsy_s.at[r, d, t, q], rsy_r.at[r, d, t, q], to)

    def rsz(r, k, e, arriving=False):
        src = z_out.at[r, z_at(k), (c + e) % C]
        dst = z_in.at[r, z_at(-k), (c + e) % C] if arriving else z_in.at[r, z, c]
        return send(src, dst, rsz_s.at[r, k, e], rsz_r.at[r, k, e], dev(s, y, z_at(k), (c + e) % C))

    def far():
        return send(far_out, far_in, far_s, far_r, dev(SECTIONS - 1 - s, y, z, c))

    def reduce(r):
        xc(r, True).wait_recv()
        for i in range(MICRO):
            dc(r, i, True).wait_recv()
        xs = x[r].reshape(C * ROWS, D)
        ds = jnp.concatenate([delta[r, 0, c], delta[r, 1, c]], axis=0)
        product = lax.dot_general(xs, ds, (((0,), (0,)), ((), ())), preferred_element_type=F32)
        part[...] = product.reshape(Y, Z, C * SHARD, H)
        for t in range(4):
            for arrived in (False, True):
                for q in range(Z):
                    for d in range(2):
                        sign = 1 - 2 * d
                        mine = part.at[y_at(sign * (4 - t)), q]
                        first = t == 0 or (t == 1 and q not in HALF[d])
                        if first == arrived or (t == 0 and q not in HALF[d]):
                            continue
                        if first:
                            y_own[r, d, q] = mine[...].astype(BF16)
                        else:
                            rsy(r, d, t - 1, q).wait_recv()
                            y_in[r, d, t - 1, q] = (y_in[r, d, t - 1, q].astype(F32) + mine[...]).astype(BF16)
                        rsy(r, d, t, q).start()
        for q in range(Z):
            for d in range(2):
                rsy(r, d, 3, q).wait_recv()
            total_q = part[y, q] + y_in[r, 0, 3, q].astype(F32) + y_in[r, 1, 3, q].astype(F32)
            z_out[r, q] = total_q.astype(BF16).reshape(C, SHARD, H)
        for k in range(Z):
            for e in range(C):
                if k or e:
                    rsz(r, k, e).start()
        z_in[r, z, c] = z_out[r, z, c]
        for k in range(Z):
            for e in range(C):
                if k or e:
                    rsz(r, k, e, True).wait_recv()
        for h in range(C):
            total[r, :, h * H : (h + 1) * H] = sum(z_in[r, q, h].astype(F32) for q in range(Z))

        @pl.when(hi == r)
        def _():
            far_out[...] = total[r].astype(BF16)
            far().start()

    def reduce_sends_done(r):
        for i in range(MICRO):
            dc(r, i).wait_send()
        for d in range(2):
            for t in range(4):
                for q in range(Z):
                    if t > 0 or q in HALF[d]:
                        rsy(r, d, t, q).wait_send()
        for k in range(Z):
            for e in range(C):
                if k or e:
                    rsz(r, k, e).wait_send()

    for r in range(2):
        own_weight(r).start()
    loads()
    barrier = pltpu.get_barrier_semaphore()
    greeted = [sibling, dev(s, y_at(1), z, c), dev(s, y_at(-1), z, c)]
    greeted += [dev(s, y, z_at(k), cc) for k in range(1, Z) for cc in (c, 1 - c)]
    greeted += [
        dev((s + 1) % SECTIONS, y, z, c),
        dev((s + SECTIONS - 1) % SECTIONS, y, z, c),
        dev(SECTIONS - 1 - s, y, z, c),
    ]
    for device in greeted:
        pl.semaphore_signal(barrier, inc=1, device_id=device, device_id_type=MESH)
    pl.semaphore_wait(barrier, len(greeted))

    ag_z_start(0)
    ag_z_start(1)
    ag_y_start(0)
    for r in range(2):
        pltpu.make_async_copy(x_down, x.at[r, c], load_sem.at[r]).wait()
        xc(r).start()
    ag_y_forward(0)
    ag_y_start(1)
    prepare(0)

    def second_weight():
        ag_y_forward(1)
        prepare(1)

    pl.when(p >= 2)(second_weight)
    chain(0)
    store_grads(0)

    @pl.when(p < 2)
    def _():
        second_weight()
        reduce(0)

    chain(1)
    store_grads(1)

    @pl.when(p >= 2)
    def _():
        reduce(0)

    reduce(1)

    far().wait_recv()
    gw[...] = (total[1 - hi] + far_in[...].astype(F32)) * (1.0 / math.sqrt(2.0 * Y * Z * C * ROWS))
    copy = pltpu.make_async_copy(gw, grad_w, out_sem.at[2])
    copy.start()
    for r in range(2):
        ag_sends_done(r)
        xc(r).wait_send()
        reduce_sends_done(r)
        for i in range(MICRO):
            if r == 0:
                hop(r, i).wait_send()
            else:
                pl.when(p > 0)(hop(r, i).wait_send)
        store_grads(r, True)
    far().wait_send()
    copy.wait()


def per_device(x_down, x_up, weights, cot_down, cot_up):
    dma = pltpu.SemaphoreType.DMA
    anywhere = pl.BlockSpec(memory_space=pl.ANY)
    grad_down, grad_up, grad_w = pl.pallas_call(
        kernel,
        out_shape=(
            jax.ShapeDtypeStruct((ROWS, D), BF16),
            jax.ShapeDtypeStruct((ROWS, D), BF16),
            jax.ShapeDtypeStruct((SHARD, D), F32),
        ),
        in_specs=[anywhere] * 5,
        out_specs=(anywhere,) * 3,
        scratch_shapes=[
            pltpu.VMEM((2, Y, Z, C, SHARD, D), BF16),
            pltpu.VMEM((2, C, ROWS, D), BF16),
            pltpu.VMEM((2, ROWS, D), BF16),
            pltpu.VMEM((2, ROWS, D), BF16),
            pltpu.VMEM((2, ROWS, D), F32),
            pltpu.VMEM((2, C, 2, ROWS, H), BF16),
            pltpu.VMEM((Y, Z, C * SHARD, H), F32),
            pltpu.VMEM((2, 2, 4, Z, C * SHARD, H), BF16),
            pltpu.VMEM((2, 2, Z, C * SHARD, H), BF16),
            pltpu.VMEM((2, Z, C, SHARD, H), BF16),
            pltpu.VMEM((2, Z, C, SHARD, H), BF16),
            pltpu.VMEM((2, SHARD, D), F32),
            pltpu.VMEM((SHARD, D), BF16),
            pltpu.VMEM((SHARD, D), BF16),
            pltpu.VMEM((SHARD, D), F32),
            dma((4,)), dma((3,)),
            dma((2, 3)), dma((2, 3)), dma((2, 2, 4, Z)), dma((2, 2, 4, Z)), dma((2, 8)), dma((2, 8)),
            dma((2,)), dma((2,)), dma((2, MICRO)), dma((2, MICRO)), dma((2, MICRO)), dma((2, MICRO)),
            dma((2, 2, 4, Z)), dma((2, 2, 4, Z)), dma((2, Z, C)), dma((2, Z, C)), dma, dma,
        ],
        compiler_params=pltpu.CompilerParams(
            collective_id=0, has_side_effects=True, vmem_limit_bytes=40 << 20
        ),
        cost_estimate=pl.CostEstimate(
            flops=3 * 2 * 2 * ROWS * D * D, bytes_accessed=4 << 20, transcendentals=4 * ROWS * D
        ),
    )(x_down[0], x_up[0], weights[0], cot_down, cot_up)
    return grad_down[None], grad_up[None], grad_w[None]


def solution(mesh):
    in_specs = (
        P("section", "dp", None),
        P("section", "dp", None),
        P("section", None, "dp", None),
        P("dp", None),
        P("dp", None),
    )
    out_specs = (P("section", "dp", None), P("section", "dp", None), P("section", "dp", None))
    return jax.shard_map(
        per_device, mesh=mesh, in_specs=in_specs, out_specs=out_specs, check_vma=False
    )
```

time: 731 us -> 131 us (0.18)
  the two profiles are of different devices: /device:TPU:6 before, /device:TPU:4 now
where the time goes in v1:
time: 131 us; the launch traced here: 130 us
  Pallas kernels  123 us (94%)
  local copies, waits for them, and re-layouts  6.67 us (5%)
    pallas_call x1, Pallas kernels, per_device(): pl.pallas_call(kernel, out_shape=(jax.ShapeDtypeStruct((ROWS, D), BF16),...  123 us
    unnamed x13, local copies, waits for them, and re-layouts  6.67 us

profile of v1, /device:TPU:4, one launch (start us, length us, event | category | flops | bytes accessed | tf_op | source)
XLA Modules:
  0.0 130.5 jit_solution(16159671445094895481)
XLA Ops:
  0.6 0.0 copy-start
  0.6 0.9 copy-done
  1.6 0.0 copy-start.1
  1.6 0.9 copy-done.1
  2.5 0.0 copy-start.2
  2.5 0.9 copy-done.2
  3.5 0.0 copy-start.3
  3.5 0.9 copy-done.3
  4.4 0.0 copy-start.4
  4.4 0.8 copy-done.4
  5.3 123.2 %shard_map.76 = (bf16[128,1024]{1,0:T(8,128)(2,1)S(1)}, bf16[128,1024]{1,0:T(8,128)(2,1)S(1)}, f32[16,1024]{1,0:T(8,128)S(1)}) custom-call(bf16[128,1024]{1,0:T(8,128)(2,1)S(1)} %bitcast.9, bf16[128,1024]{1,0:T(8,128)(2,1)S(1)} %bitcast.10, bf16[2,16,1024]{2,1,0:T(8,128)(2,1)S(1)} %bitcast.11, bf16[128,1024]{1,0:T(8,128)(2,1)S(1)} %copy-done.2, ...), custom_call_target="tpu_custom_call" | custom-call | flops 1610612736 | bytes 4194304 | tf_op jit(solution)/shard_map/pallas_call | solution.py:343
  128.5 0.7 copy.11
  129.2 0.7 copy.12
  129.9 0.6 copy.13
Async XLA Ops:
  0.6 1.0 copy-start
  1.6 0.9 copy-start.1
  2.5 0.9 copy-start.2
  3.5 0.9 copy-start.3
  4.4 0.8 copy-start.4
